TPU v7x, 32 devices: a whole 2x2x4 slice. The times are simulated.
32 devices in a mesh: runs: 2 (over y), ens: 2 (over core), space: 8 (over z, x).
Axes of the slice: x: 2, y: 2, z: 4, core: 2. Of those that a mesh axis runs over, the one named last changes fastest.
Arguments:
- analysis: float32 [8, 8, 64, 3600], P(('runs', 'ens'), None, 'space'), parts along dimension 0, may hold values from -6 to 6
- copy_counts: int32 [8], P('runs'), parts along dimension 0, may hold values from 0 to 3, as said below
- spreading_coefficient: float32 [128, 3600], P(('runs', 'space')), parts along dimension 0, may hold values from 0.04 to 0.2
- component_interaction: float32 [8, 8], replicated, may hold values from -0.3 to 0.3
- ocean_mask: int32 [128, 3600], P(('runs', 'space')), parts along dimension 0, may hold values 0 or 1
- measured_grid_location: int32 [8192], P(('runs', 'space')), parts along dimension 0, may hold values from 0 to 28799
- measured_surface_reading: float32 [8192], P(('runs', 'space')), parts along dimension 0, may hold values from -6 to 6
- measured_inverse_variance: float32 [8192], P(('runs', 'space')), parts along dimension 0, may hold values from 0.3 to 27, as said below
Outputs:
- predicted_ensemble: float32 [8, 8, 64, 3600], P(('runs', 'ens'), None, 'space'), parts along dimension 0
- average_fit_score: float32 [8], P(('runs', 'ens')), parts along dimension 0
There are 2 independent parts, one for each index of `runs`. A program takes and returns all parts, laid end to end along the dimension named above; an argument that names none is the same for every part. Nothing has to cross between parts.
Inputs may be any that keep to these rules, and one draw needn't show every extreme that they name: `copy_counts`: the counts sum to 4; one particle gets exactly 3 copies; the particles of the first ens slot together get a count other than 2. `measured_inverse_variance`: Positive.
All inputs are finite; a program needn't handle non-finite values. No bound on the sum of `ocean_mask` on one device may be relied on, other than what follows from the above.
Results may differ from a plain program's by a relative error of at most 0.00011.
Values sent between devices are 32-bit elements; how exact they have to be, the bound alone decides.
A program may use at most 64 MiB of HBM per device.

v0:
```python
import jax
import jax.numpy as jnp
from jax import lax
from jax.sharding import PartitionSpec as P

SUBSTEPS = 3


def padded_2(value, sides, width):
    for axis, dim in sides:
        peers, length = (lax.axis_size(axis), value.shape[dim])
        up = [(i, (i + 1) % peers) for i in range(peers - 1)]
        down = [(j, i) for i, j in up]
        last = lax.slice_in_dim(value, length - width, length, axis=dim)
        leading = lax.slice_in_dim(value, 0, width, axis=dim)
        before = lax.ppermute(last, axis, up)
        after = lax.ppermute(leading, axis, down)
        value = jnp.concatenate([before, value, after], axis=dim)
    return value


def update(padded, spreading_coefficient, water_grid_flag, component_interaction):
    centre = padded[:, :, 1:-1]
    laplace = (
        padded[:, :, 2:]
        + padded[:, :, :-2]
        + jnp.roll(centre, -1, axis=3)
        + jnp.roll(centre, 1, axis=3)
        - 4.0 * centre
    )
    mixing = jnp.einsum(
        "ij,pjrc->pirc", component_interaction, centre, precision=lax.Precision.HIGHEST
    )
    return water_grid_flag * (centre + spreading_coefficient * laplace + mixing)


def advance_model_time(fields, spreading_coefficient, water_grid_flag, component_interaction):
    current = fields
    for substep in range(SUBSTEPS):
        padded = padded_2(current, (("space", 2),), 1)
        current = update(padded, spreading_coefficient, water_grid_flag, component_interaction)
    return current


def particle_likelihood(
    fields, measured_grid_location, measured_surface_reading, measured_inverse_variance
):
    per_slot = fields.shape[0]
    surface = fields[:, 0].reshape(per_slot, -1)
    picked = jnp.take(surface, measured_grid_location, axis=1)
    misfit = picked - measured_surface_reading[None, :]
    partial_value = jnp.sum(measured_inverse_variance[None, :] * misfit * misfit, axis=1)
    summed = lax.psum(partial_value, "space")
    obs_total = measured_surface_reading.shape[0] * lax.axis_size("space")
    return -0.5 * summed / obs_total


def body(
    analysis,
    copy_counts,
    spreading_coefficient,
    component_interaction,
    ocean_mask,
    measured_grid_location,
    measured_surface_reading,
    measured_inverse_variance,
):
    per_slot = analysis.shape[0]
    water_grid_flag = ocean_mask.astype(jnp.float32)
    bounds = jnp.cumsum(copy_counts)
    position = jnp.arange(copy_counts.shape[0], dtype=jnp.int32)
    parents = jnp.sum((bounds[None, :] <= position[:, None]).astype(jnp.int32), axis=1)
    my_parents = lax.dynamic_slice_in_dim(parents, lax.axis_index("ens") * per_slot, per_slot)
    everyone = lax.all_gather(analysis, "ens", axis=0, tiled=True)
    starting_ensemble = jnp.take(everyone, my_parents, axis=0)
    predicted_ensemble = advance_model_time(
        starting_ensemble, spreading_coefficient, water_grid_flag, component_interaction
    )
    average_fit_score = particle_likelihood(
        predicted_ensemble,
        measured_grid_location,
        measured_surface_reading,
        measured_inverse_variance,
    )
    return (predicted_ensemble, average_fit_score)


def solution(mesh):
    in_specs = (
        P(("runs", "ens"), None, "space", None),
        P("runs"),
        P(("runs", "space"), None),
        P(),
        P(("runs", "space"), None),
        P(("runs", "space")),
        P(("runs", "space")),
        P(("runs", "space")),
    )
    out_specs = (P(("runs", "ens"), None, "space", None), P(("runs", "ens")))
    return jax.shard_map(body, mesh=mesh, in_specs=in_specs, out_specs=out_specs, check_vma=False)
```

profile of v0, /device:TPU:0, one launch (start us, length us, event | category | flops | bytes accessed | tf_op | source)
XLA Modules:
  0.0 126.7 jit_solution(3646494042270901811)
XLA Ops:
  7.3 0.7 all-gather.2.cloned.1.call-update
  8.0 0.2 reduce-window.8
  8.2 0.1 convert_reduce_fusion
  8.3 0.1 compare_and_fusion.1
  8.4 17.0 %all-gather.2.cloned.1.call-done = f32[4,8,8,3600]{3,2,1,0:T(8,128)} async-done(((f32[2,8,8,3600]{3,2,1,0:T(8,128)}), f32[4,8,8,3600]{3,2,1,0:T(8,128)}) %all-gather.2.cloned.1.call-update) | async-done | bytes 3686416 | tf_op jit(solution)/shard_map/all_gather | solution.py:74
  25.4 2.7 %gather_fusion = f32[2,8,8,3600]{3,2,1,0:T(8,128)S(1)} fusion(f32[4,8,8,3600]{3,2,1,0:T(8,128)} %all-gather.2.cloned.1.call-done, s32[1024]{0:T(1024)S(1)} %pad_clamp_fusion.1), kind=kCustom, calls=%fused_computation | custom fusion | bytes 3686408 | tf_op jit(solution)/shard_map/jit(_take)/gather | solution.py:75
  28.2 0.5 copy_select_fusion
  28.7 1.3 %collective-permute-start = (f32[2,8,1,3600]{3,1,2,0:T(8,128)S(1)}, f32[2,8,1,3600]{3,1,2,0:T(8,128)S(1)}, u32[]{:S(2)}, u32[]{:S(2)}) collective-permute-start(f32[2,8,1,3600]{3,1,2,0:T(8,128)S(1)} %get-tuple-element.28), channel_id=1, source_target_pairs={{1,0},{2,1},{3,2},{4,3},{5,4},{6,5},{7,6},{9,8},{10,9},{11,10},{12... | collective-permute-start | bytes 691208 | tf_op jit(solution)/shard_map/ppermute | solution.py:17
  30.0 4.7 %collective-permute-start.1 = (f32[2,8,1,3600]{3,1,2,0:T(8,128)S(1)}, f32[2,8,1,3600]{3,1,2,0:T(8,128)S(1)}, u32[]{:S(2)}, u32[]{:S(2)}) collective-permute-start(f32[2,8,1,3600]{3,1,2,0:T(8,128)S(1)} %get-tuple-element.29), channel_id=1, source_target_pairs={{0,1},{1,2},{2,3},{3,4},{4,5},{5,6},{6,7},{8,9},{9,10},{10,11},{11... | collective-permute-start | bytes 691208 | tf_op jit(solution)/shard_map/ppermute | solution.py:16
  34.7 0.6 fusion.35
  35.4 3.2 %collective-permute-done = f32[2,8,1,3600]{3,1,2,0:T(8,128)S(1)} collective-permute-done((f32[2,8,1,3600]{3,1,2,0:T(8,128)S(1)}, f32[2,8,1,3600]{3,1,2,0:T(8,128)S(1)}, u32[]{:S(2)}, u32[]{:S(2)}) %collective-permute-start) | collective-permute-done | bytes 230432 | tf_op jit(solution)/shard_map/ppermute | solution.py:17
  38.6 5.2 %collective-permute-done.1 = f32[2,8,1,3600]{3,1,2,0:T(8,128)S(1)} collective-permute-done((f32[2,8,1,3600]{3,1,2,0:T(8,128)S(1)}, f32[2,8,1,3600]{3,1,2,0:T(8,128)S(1)}, u32[]{:S(2)}, u32[]{:S(2)}) %collective-permute-start.1) | collective-permute-done | bytes 230432 | tf_op jit(solution)/shard_map/ppermute | solution.py:16
  43.8 2.9 %fusion.5 = f32[2,8,8,3600]{3,1,2,0:T(8,128)S(1)} fusion(f32[2,8,8,3600]{3,1,2,0:T(8,128)S(1)} %copy_select_fusion, f32[2,8,1,3600]{3,1,2,0:T(8,128)S(1)} %collective-permute-done.1, f32[2,8,1,3600]{3,1,2,0:T(8,128)S(1)} %collective-permute-done, f32[2,8,8,1]{3,1,2,0:T(8,128)S(1)} %get-tuple-element.25, f32[2,8,8,3599]{3,1,2,0:T(8,128)S(1)} %get-tuple-element.27, ...), kind=kOutput, calls=%fused_computation.10 | convolution fusion | flops 50227200 | bytes 8064256 | tf_op jit(solution)/shard_map/ij,pjrc->pirc/dot_general | solution.py:31
  46.7 1.3 %collective-permute-start.2 = (f32[2,8,1,3600]{3,1,2,0:T(8,128)S(1)}, f32[2,8,1,3600]{3,1,2,0:T(8,128)S(1)}, u32[]{:S(2)}, u32[]{:S(2)}) collective-permute-start(f32[2,8,1,3600]{3,1,2,0:T(8,128)S(1)} %get-tuple-element.22), channel_id=1, source_target_pairs={{1,0},{2,1},{3,2},{4,3},{5,4},{6,5},{7,6},{9,8},{10,9},{11,10},{12... | collective-permute-start | bytes 691208 | tf_op jit(solution)/shard_map/ppermute | solution.py:17
  48.0 5.0 %collective-permute-start.3 = (f32[2,8,1,3600]{3,1,2,0:T(8,128)S(1)}, f32[2,8,1,3600]{3,1,2,0:T(8,128)S(1)}, u32[]{:S(2)}, u32[]{:S(2)}) collective-permute-start(f32[2,8,1,3600]{3,1,2,0:T(8,128)S(1)} %get-tuple-element.23), channel_id=1, source_target_pairs={{0,1},{1,2},{2,3},{3,4},{4,5},{5,6},{6,7},{8,9},{9,10},{10,11},{11... | collective-permute-start | bytes 691208 | tf_op jit(solution)/shard_map/ppermute | solution.py:16
  53.1 0.6 fusion.32
  53.8 3.3 %collective-permute-done.2 = f32[2,8,1,3600]{3,1,2,0:T(8,128)S(1)} collective-permute-done((f32[2,8,1,3600]{3,1,2,0:T(8,128)S(1)}, f32[2,8,1,3600]{3,1,2,0:T(8,128)S(1)}, u32[]{:S(2)}, u32[]{:S(2)}) %collective-permute-start.2) | collective-permute-done | bytes 230432 | tf_op jit(solution)/shard_map/ppermute | solution.py:17
  57.1 5.2 %collective-permute-done.3 = f32[2,8,1,3600]{3,1,2,0:T(8,128)S(1)} collective-permute-done((f32[2,8,1,3600]{3,1,2,0:T(8,128)S(1)}, f32[2,8,1,3600]{3,1,2,0:T(8,128)S(1)}, u32[]{:S(2)}, u32[]{:S(2)}) %collective-permute-start.3) | collective-permute-done | bytes 230432 | tf_op jit(solution)/shard_map/ppermute | solution.py:16
  62.3 2.9 %fusion.3 = f32[2,8,8,3600]{3,1,2,0:T(8,128)S(1)} fusion(f32[2,8,8,3600]{3,1,2,0:T(8,128)S(1)} %fusion.5, f32[2,8,1,3600]{3,1,2,0:T(8,128)S(1)} %collective-permute-done.3, f32[2,8,1,3600]{3,1,2,0:T(8,128)S(1)} %collective-permute-done.2, f32[2,8,8,1]{3,1,2,0:T(8,128)S(1)} %get-tuple-element.19, f32[2,8,8,3599]{3,1,2,0:T(8,128)S(1)} %get-tuple-element.21, ...), kind=kOutput, calls=%fused_computation.7 | convolution fusion | flops 50227200 | bytes 8064256 | tf_op jit(solution)/shard_map/ij,pjrc->pirc/dot_general | solution.py:31
  65.3 1.3 %collective-permute-start.4 = (f32[2,8,1,3600]{3,1,2,0:T(8,128)S(1)}, f32[2,8,1,3600]{3,1,2,0:T(8,128)S(1)}, u32[]{:S(2)}, u32[]{:S(2)}) collective-permute-start(f32[2,8,1,3600]{3,1,2,0:T(8,128)S(1)} %get-tuple-element.16), channel_id=1, source_target_pairs={{1,0},{2,1},{3,2},{4,3},{5,4},{6,5},{7,6},{9,8},{10,9},{11,10},{12... | collective-permute-start | bytes 691208 | tf_op jit(solution)/shard_map/ppermute | solution.py:17
  66.6 5.2 %collective-permute-start.5 = (f32[2,8,1,3600]{3,1,2,0:T(8,128)S(1)}, f32[2,8,1,3600]{3,1,2,0:T(8,128)S(1)}, u32[]{:S(2)}, u32[]{:S(2)}) collective-permute-start(f32[2,8,1,3600]{3,1,2,0:T(8,128)S(1)} %get-tuple-element.17), channel_id=1, source_target_pairs={{0,1},{1,2},{2,3},{3,4},{4,5},{5,6},{6,7},{8,9},{9,10},{10,11},{11... | collective-permute-start | bytes 691208 | tf_op jit(solution)/shard_map/ppermute | solution.py:16
  71.8 0.6 fusion.29
  72.5 3.1 %collective-permute-done.4 = f32[2,8,1,3600]{3,1,2,0:T(8,128)S(1)} collective-permute-done((f32[2,8,1,3600]{3,1,2,0:T(8,128)S(1)}, f32[2,8,1,3600]{3,1,2,0:T(8,128)S(1)}, u32[]{:S(2)}, u32[]{:S(2)}) %collective-permute-start.4) | collective-permute-done | bytes 230432 | tf_op jit(solution)/shard_map/ppermute | solution.py:17
  75.6 5.2 %collective-permute-done.5 = f32[2,8,1,3600]{3,1,2,0:T(8,128)S(1)} collective-permute-done((f32[2,8,1,3600]{3,1,2,0:T(8,128)S(1)}, f32[2,8,1,3600]{3,1,2,0:T(8,128)S(1)}, u32[]{:S(2)}, u32[]{:S(2)}) %collective-permute-start.5) | collective-permute-done | bytes 230432 | tf_op jit(solution)/shard_map/ppermute | solution.py:16
  80.8 2.9 %fusion.1 = f32[2,8,8,3600]{3,1,2,0:T(8,128)S(1)} fusion(f32[2,8,8,3600]{3,1,2,0:T(8,128)S(1)} %fusion.3, f32[2,8,1,3600]{3,1,2,0:T(8,128)S(1)} %collective-permute-done.5, f32[2,8,1,3600]{3,1,2,0:T(8,128)S(1)} %collective-permute-done.4, f32[2,8,8,1]{3,1,2,0:T(8,128)S(1)} %get-tuple-element.13, f32[2,8,8,3599]{3,1,2,0:T(8,128)S(1)} %get-tuple-element.15, ...), kind=kOutput, calls=%fused_computation.4 | convolution fusion | flops 50227200 | bytes 8064256 | tf_op jit(solution)/shard_map/ij,pjrc->pirc/dot_general | solution.py:31
  83.7 0.1 slice.132
  83.9 7.7 %copy.22 = f32[2,1,8,3600]{0,3,2,1:T(8,128)} copy(f32[2,1,8,3600]{3,1,2,0:T(1,128)S(1)} %slice.132) | data formatting | bytes 460800 | tf_op jit(solution)/shard_map/reshape;squeeze | solution.py:49
  91.6 6.2 %gather_fusion.1 = f32[512,2]{1,0:T(8,128)S(1)} fusion(f32[2,28800]{0,1:T(8,128)} %bitcast.35, s32[1024]{0:T(1024)S(1)} %pad_clamp_fusion), kind=kCustom, calls=%fused_computation.1 | custom fusion | bytes 10240 | tf_op jit(solution)/shard_map/jit(_take)/gather | solution.py:50
  97.8 0.3 fusion.24
  98.1 1.6 %copy.20 = f32[2,8,8,3600]{3,2,1,0:T(8,128)} copy(f32[2,8,8,3600]{3,1,2,0:T(8,128)S(1)} %fusion.1) | data formatting | bytes 3686400
  99.7 19.6 %psum.7 = f32[2]{0:T(128)S(1)} all-reduce(f32[2]{0:T(128)S(1)} %fusion.24), channel_id=1, replica_groups=mesh['runs'=2,'ens'=2,'space'=8] {'space'}, use_global_device_ids=true, to_apply=%region_3.4 | all-reduce | flops 2 | bytes 16 | tf_op jit(solution)/shard_map/psum | solution.py:53
  119.4 0.5 broadcast_multiply_fusion
  (26 shorter events, 0.5 us)
Async XLA Ops:
  7.2 36.6 %copy-start = (f32[8,8]{1,0:T(8,128)S(1)}, f32[8,8]{1,0:T(8,128)}, u32[]{:S(2)}) copy-start(f32[8,8]{1,0:T(8,128)} %param.11) | copy-start | bytes 772
  7.2 0.8 copy-start.6
  7.2 1.0 copy-start.1
  7.2 1.2 copy-start.2
  7.2 18.2 %all-gather.2.cloned.1.call-start = ((), (), s32[]{:S(2)}) async-start(), calls=%async_computation | async-start | bytes 5701632 | tf_op jit(solution)/shard_map/all_gather | solution.py:74
  28.7 9.9 %collective-permute-start = (f32[2,8,1,3600]{3,1,2,0:T(8,128)S(1)}, f32[2,8,1,3600]{3,1,2,0:T(8,128)S(1)}, u32[]{:S(2)}, u32[]{:S(2)}) collective-permute-start(f32[2,8,1,3600]{3,1,2,0:T(8,128)S(1)} %get-tuple-element.28), channel_id=1, source_target_pairs={{1,0},{2,1},{3,2},{4,3},{5,4},{6,5},{7,6},{9,8},{10,9},{11,10},{12... | collective-permute-start | bytes 691208 | tf_op jit(solution)/shard_map/ppermute | solution.py:17
  30.0 13.8 %copy-start.5 = (f32[8,3600]{1,0:T(8,128)S(1)}, f32[8,3600]{1,0:T(8,128)}, u32[]{:S(2)}) copy-start(f32[8,3600]{1,0:T(8,128)} %param.10) | copy-start | bytes 345604
  30.0 13.8 %collective-permute-start.1 = (f32[2,8,1,3600]{3,1,2,0:T(8,128)S(1)}, f32[2,8,1,3600]{3,1,2,0:T(8,128)S(1)}, u32[]{:S(2)}, u32[]{:S(2)}) collective-permute-start(f32[2,8,1,3600]{3,1,2,0:T(8,128)S(1)} %get-tuple-element.29), channel_id=1, source_target_pairs={{0,1},{1,2},{2,3},{3,4},{4,5},{5,6},{6,7},{8,9},{9,10},{10,11},{11... | collective-permute-start | bytes 691208 | tf_op jit(solution)/shard_map/ppermute | solution.py:16
  46.7 10.3 %collective-permute-start.2 = (f32[2,8,1,3600]{3,1,2,0:T(8,128)S(1)}, f32[2,8,1,3600]{3,1,2,0:T(8,128)S(1)}, u32[]{:S(2)}, u32[]{:S(2)}) collective-permute-start(f32[2,8,1,3600]{3,1,2,0:T(8,128)S(1)} %get-tuple-element.22), channel_id=1, source_target_pairs={{1,0},{2,1},{3,2},{4,3},{5,4},{6,5},{7,6},{9,8},{10,9},{11,10},{12... | collective-permute-start | bytes 691208 | tf_op jit(solution)/shard_map/ppermute | solution.py:17
  48.0 14.3 %collective-permute-start.3 = (f32[2,8,1,3600]{3,1,2,0:T(8,128)S(1)}, f32[2,8,1,3600]{3,1,2,0:T(8,128)S(1)}, u32[]{:S(2)}, u32[]{:S(2)}) collective-permute-start(f32[2,8,1,3600]{3,1,2,0:T(8,128)S(1)} %get-tuple-element.23), channel_id=1, source_target_pairs={{0,1},{1,2},{2,3},{3,4},{4,5},{5,6},{6,7},{8,9},{9,10},{10,11},{11... | collective-permute-start | bytes 691208 | tf_op jit(solution)/shard_map/ppermute | solution.py:16
  65.3 10.3 %collective-permute-start.4 = (f32[2,8,1,3600]{3,1,2,0:T(8,128)S(1)}, f32[2,8,1,3600]{3,1,2,0:T(8,128)S(1)}, u32[]{:S(2)}, u32[]{:S(2)}) collective-permute-start(f32[2,8,1,3600]{3,1,2,0:T(8,128)S(1)} %get-tuple-element.16), channel_id=1, source_target_pairs={{1,0},{2,1},{3,2},{4,3},{5,4},{6,5},{7,6},{9,8},{10,9},{11,10},{12... | collective-permute-start | bytes 691208 | tf_op jit(solution)/shard_map/ppermute | solution.py:17
  66.6 14.3 %collective-permute-start.5 = (f32[2,8,1,3600]{3,1,2,0:T(8,128)S(1)}, f32[2,8,1,3600]{3,1,2,0:T(8,128)S(1)}, u32[]{:S(2)}, u32[]{:S(2)}) collective-permute-start(f32[2,8,1,3600]{3,1,2,0:T(8,128)S(1)} %get-tuple-element.17), channel_id=1, source_target_pairs={{0,1},{1,2},{2,3},{3,4},{4,5},{5,6},{6,7},{8,9},{9,10},{10,11},{11... | collective-permute-start | bytes 691208 | tf_op jit(solution)/shard_map/ppermute | solution.py:16
  83.9 13.9 %copy-start.3 = (f32[512]{0:T(512)S(1)}, f32[512]{0:T(512)}, u32[]{:S(2)}) copy-start(f32[512]{0:T(512)} %param.14) | copy-start | bytes 6148
  83.9 13.9 %copy-start.4 = (f32[512]{0:T(512)S(1)}, f32[512]{0:T(512)}, u32[]{:S(2)}) copy-start(f32[512]{0:T(512)} %param.15) | copy-start | bytes 6148
Sparse Core Ops, SparseCore 0:
  9.6 15.7 all-gather.1
where the time goes:
time: 127 us
  waiting for transfers between devices  43 us (34%)
  local copies, waits for them, and re-layouts  20.6 us (16%)
  blocking collectives  19.6 us (15%)
  starting transfers between devices  18.8 us (15%)
  between operations  14.3 us (11%)
  matrix products  8.65 us (7%)
  other arithmetic  1.69 us (1%)
    psum x1, blocking collectives, particle_likelihood(): summed = lax.psum(partial_value, 'space')  19.6 us
    all_gather x1, waiting for transfers between devices, body(): everyone = lax.all_gather(analysis, 'ens', axis=0, tiled=True)  17 us
    ppermute x3, waiting for transfers between devices, padded_2(): before = lax.ppermute(last, axis, up)  15.7 us
    ppermute x3, starting transfers between devices, padded_2(): before = lax.ppermute(last, axis, up)  14.9 us
    ppermute x3, waiting for transfers between devices, padded_2(): after = lax.ppermute(leading, axis, down)  9.63 us
    dot_general x3, matrix products, update(): jnp.einsum('ij,pjrc->pirc', component_interaction, centre, precision=lax....  8.65 us
    another operation x1, local copies, waits for them, and re-layouts, particle_likelihood(): surface = fields[:, 0].reshape(per_slot, -1)  7.68 us
    gather x1, local copies, waits for them, and re-layouts, particle_likelihood(): picked = jnp.take(surface, measured_grid_location, axis=1)  6.22 us
  transfers between devices with their start and end apart: 7, of which 7 were waited for; matrix products, arithmetic and copies ran while one was open for 2% of the time, Pallas kernels for 0%

commit v1 on v0

v1 whole, which is shorter than its diff:
```python
import functools

import jax
import jax.numpy as jnp
from jax import lax
from jax.experimental import pallas as pl
from jax.experimental.pallas import tpu as pltpu
from jax.sharding import PartitionSpec as P

SUBSTEPS = 3
CHUNKS = 4
LANES = 128
MESH = pl.DeviceIdType.MESH


def radix_steps(peers):
    steps, stride = [], 1
    while peers > 1:
        size = 8 if peers % 8 == 0 else (peers if peers < 8 else 2 if peers % 2 == 0 else peers)
        steps.append((stride, size))
        stride, peers = stride * size, peers // size
    return steps


def forecast_kernel(
    peers,
    counts,
    inter,
    analysis,
    coef,
    mask,
    loc,
    reading,
    inv_var,
    out,
    totals,
    raw,
    cand,
    taken,
    edges,
    send,
    north,
    south,
    fields,
    result,
    other,
    wet,
    wcoef,
    surface,
    pair,
    gather,
    load_sem,
    edge_sem,
    cand_sem,
    send_sem,
    recv_sem,
    final_send,
    final_recv,
    store_sem,
    pair_sem,
    sum_send,
    sum_recv,
):
    comp, rows, lon = analysis.shape[1:]
    tiles = wet.shape[1] // LANES
    slots = counts.shape[0]
    per_slot = slots // 2
    tail = lon - (tiles - 1) * LANES
    half = (LANES - tail) // 2
    bounds = [tiles * j // CHUNKS for j in range(CHUNKS + 1)]
    steps = radix_steps(peers)

    e = lax.axis_index("ens")
    me = lax.axis_index("space")
    has_north = me > 0
    has_south = me < peers - 1

    loads = [
        pltpu.make_async_copy(analysis.at[p], raw.at[p], load_sem.at[p]) for p in range(per_slot)
    ]
    for copy in loads:
        copy.start()

    def digit_peers():
        for r, (stride, size) in enumerate(steps):
            digit = lax.rem(me // stride, size)
            for q in range(1, size):
                to = lax.rem(digit + q, size)
                yield r, q, digit, to, me + (to - digit) * stride

    barrier = pltpu.get_barrier_semaphore()
    pl.semaphore_signal(barrier, inc=1, device_id={"ens": 1 - e}, device_id_type=MESH)
    waits = 1
    for r, q, digit, to, dev in digit_peers():
        pl.semaphore_signal(barrier, inc=1, device_id={"space": dev}, device_id_type=MESH)
        waits += 1

    if len(steps) > 1:

        @pl.when(has_north)
        def _():
            pl.semaphore_signal(barrier, inc=1, device_id={"space": me - 1}, device_id_type=MESH)

        @pl.when(has_south)
        def _():
            pl.semaphore_signal(barrier, inc=1, device_id={"space": me + 1}, device_id_type=MESH)

        waits = waits + has_north.astype(jnp.int32) + has_south.astype(jnp.int32)

    def tail_of(load):
        return jnp.concatenate(
            [load(lon - tail, lon), load(0, half), load(lon - (LANES - tail - half), lon)], axis=-1
        )

    def tile_loop(first, last, body):
        def step(k, carry):
            body(k, pl.ds(pl.multiple_of(k * LANES, LANES), LANES))
            return carry

        lax.fori_loop(first, last, step, 0)

    last = pl.ds((tiles - 1) * LANES, LANES)

    def prepare(c, m, at):
        w = m.astype(jnp.float32)
        wet[:, at] = w
        wcoef[:, at] = w * c

    tile_loop(0, tiles - 1, lambda k, at: prepare(coef[:, at], mask[:, at], at))
    prepare(
        tail_of(lambda a, b: coef[:, a:b]),
        tail_of(lambda a, b: mask[:, a:b].astype(jnp.float32)),
        last,
    )
    surface[tiles * rows :, :] = jnp.zeros((surface.shape[0] - tiles * rows, LANES), jnp.float32)

    @pl.when(jnp.logical_not(has_north))
    def _():
        for s in range(SUBSTEPS):
            north[s] = jnp.zeros(north.shape[1:], jnp.float32)

    @pl.when(jnp.logical_not(has_south))
    def _():
        for s in range(SUBSTEPS):
            south[s] = jnp.zeros(south.shape[1:], jnp.float32)

    sums, total = [], 0
    for i in range(slots):
        total = total + counts[i]
        sums.append(total)
    first = sum((v <= 0).astype(jnp.int32) for v in sums)
    final = sum((v <= slots - 1).astype(jnp.int32) for v in sums)
    mine = jnp.where(e == 0, first, final)
    theirs = jnp.where(e == 0, final, first)
    is_own = mine // per_slot == e
    their_row = theirs % per_slot
    own_row = mine % per_slot
    edge_row = jnp.where(is_own, 0, 1)

    for copy in loads:
        copy.wait()

    def pack_edges(p, slot):
        def put(load, at):
            for c in range(comp):
                v = load(c)
                edges[slot, 0, c : c + 1, at] = v[0:1]
                edges[slot, 1, c : c + 1, at] = v[rows - 1 : rows]

        tile_loop(0, tiles - 1, lambda k, at: put(lambda c: raw[p, c, :, at], at))
        put(lambda c: tail_of(lambda a, b: raw[p, c, :, a:b]), last)

    pack_edges(their_row, 2)

    pl.semaphore_wait(barrier, waits)

    edge_copy = pltpu.make_async_remote_copy(
        edges.at[2], edges.at[1], edge_sem.at[0], edge_sem.at[1], {"ens": 1 - e}, MESH
    )
    edge_copy.start()
    for c in range(comp):
        cand[c] = raw[their_row, c]
    cand_copy = pltpu.make_async_remote_copy(
        cand, taken, cand_sem.at[0], cand_sem.at[1], {"ens": 1 - e}, MESH
    )
    cand_copy.start()
    pack_edges(own_row, 0)
    edge_copy.wait()

    def halo_copy(s, side, j):
        at = pl.ds(bounds[j] * LANES, (bounds[j + 1] - bounds[j]) * LANES)
        dst = south if side == 0 else north
        to = me - 1 if side == 0 else me + 1
        return pltpu.make_async_remote_copy(
            send.at[s, side, :, at],
            dst.at[s, :, at],
            send_sem.at[s, side, j],
            recv_sem.at[s, side, j],
            {"space": to},
            MESH,
        )

    def send_halo(s, j):
        @pl.when(has_north)
        def _():
            halo_copy(s, 0, j).start()

        @pl.when(has_south)
        def _():
            halo_copy(s, 1, j).start()

    for j in range(CHUNKS):

        def move(k, at):
            for side in range(2):
                send[0, side, :, at] = edges[edge_row, side, :, at]

        tile_loop(bounds[j], bounds[j + 1], move)
        send_halo(0, j)

    cand_copy.wait()

    def begin(k, at):
        for c in range(comp):
            fields[0, c, :, at] = jnp.where(is_own, raw[own_row, c, :, at], taken[c, :, at])

    tile_loop(0, tiles - 1, begin)
    for c in range(comp):
        fields[0, c, :, last] = tail_of(
            lambda a, b: jnp.where(is_own, raw[own_row, c, :, a:b], taken[c, :, a:b])
        )

    lane = lax.broadcasted_iota(jnp.int32, (rows, LANES), 1)
    row = lax.broadcasted_iota(jnp.int32, (rows, LANES), 0)

    def final_copy(j):
        at = pl.ds(bounds[j] * LANES, (bounds[j + 1] - bounds[j]) * LANES)
        return pltpu.make_async_remote_copy(
            result.at[:, :, at],
            other.at[:, :, at],
            final_send.at[j],
            final_recv.at[j],
            {"ens": 1 - e},
            MESH,
        )

    def store_copy(which, j):
        at = pl.ds(bounds[j] * LANES, (bounds[j + 1] - bounds[j]) * LANES)
        src, slot = (result, e) if which == 0 else (other, 1 - e)
        return pltpu.make_async_copy(
            src.at[:, :, at], out.at[slot, :, :, at], store_sem.at[which, j]
        )

    for s in range(SUBSTEPS):
        src = fields.at[s % 2]
        dst = result if s == SUBSTEPS - 1 else fields.at[(s + 1) % 2]
        for j in range(CHUNKS):

            @pl.when(has_north)
            def _():
                halo_copy(s, 1, j).wait_recv()

            @pl.when(has_south)
            def _():
                halo_copy(s, 0, j).wait_recv()

            def advance(k, at):
                before = pl.ds(pl.multiple_of(lax.rem(k + tiles - 1, tiles) * LANES, LANES), LANES)
                after = pl.ds(pl.multiple_of(lax.rem(k + 1, tiles) * LANES, LANES), LANES)
                x = [src[c, :, at] for c in range(comp)]
                w, wc = wet[:, at], wcoef[:, at]
                for i in range(comp):
                    mixing = x[i]
                    for c in range(comp):
                        mixing = mixing + inter[i, c] * x[c]
                    left = jnp.where(
                        lane == 0, pltpu.roll(src[i, :, before], 1, 1), pltpu.roll(x[i], 1, 1)
                    )
                    right = jnp.where(
                        lane == LANES - 1,
                        pltpu.roll(src[i, :, after], LANES - 1, 1),
                        pltpu.roll(x[i], LANES - 1, 1),
                    )
                    up = jnp.where(row == 0, north[s, i : i + 1, at], pltpu.roll(x[i], 1, 0))
                    down = jnp.where(
                        row == rows - 1, south[s, i : i + 1, at], pltpu.roll(x[i], rows - 1, 0)
                    )
                    v = w * mixing + wc * ((up + down) + (left + right) - 4.0 * x[i])
                    dst[i, :, at] = v
                    if s < SUBSTEPS - 1:
                        send[s + 1, 0, i : i + 1, at] = v[0:1]
                        send[s + 1, 1, i : i + 1, at] = v[rows - 1 : rows]
                    elif i == 0:
                        surface[pl.ds(pl.multiple_of(k * rows, rows), rows), :] = v

            tile_loop(bounds[j], bounds[j + 1], advance)
            if s < SUBSTEPS - 1:
                send_halo(s + 1, j)
            else:
                final_copy(j).start()
                store_copy(0, j).start()

    where = loc[...]
    band_row = sum((where >= lon * i).astype(jnp.int32) for i in range(1, rows))
    column = where - band_row * lon
    tile = column // LANES
    key = tile * rows + band_row
    within = column - tile * LANES
    obs = where.shape[1]
    hot = (lax.broadcasted_iota(jnp.int32, (surface.shape[0], obs), 0) == key).astype(jnp.float32)
    picked = jnp.dot(
        surface[...].T, hot, precision=lax.Precision.HIGHEST, preferred_element_type=jnp.float32
    )
    picked = jnp.sum(
        jnp.where(lax.broadcasted_iota(jnp.int32, (LANES, obs), 0) == within, picked, 0.0),
        axis=0,
        keepdims=True,
    )
    misfit = picked - reading[...]
    partial = jnp.sum(inv_var[...] * misfit * misfit, axis=1, keepdims=True)
    pair[pl.ds(e, 1)] = jnp.broadcast_to(partial[None], (1, 8, LANES))
    pair_copy = pltpu.make_async_remote_copy(
        pair.at[e], pair.at[e], pair_sem.at[0], pair_sem.at[1], {"ens": 1 - e}, MESH
    )
    pair_copy.start()
    pair_copy.wait()
    running = pair[...]
    for r, (stride, size) in enumerate(steps):
        digit = lax.rem(me // stride, size)
        gather[r, pl.ds(digit, 1)] = running[None]
        copies = [
            pltpu.make_async_remote_copy(
                gather.at[r, digit],
                gather.at[r, digit],
                sum_send.at[r, q],
                sum_recv.at[r, q],
                {"space": dev},
                MESH,
            )
            for rr, q, _, _, dev in digit_peers()
            if rr == r
        ]
        for copy in copies:
            copy.start()
        for copy in copies:
            copy.wait()
        running = gather[r, 0]
        for q in range(1, size):
            running = running + gather[r, q]
    totals[...] = running

    for j in range(CHUNKS):
        final_copy(j).wait_recv()
        store_copy(1, j).start()
    for j in range(CHUNKS):
        final_copy(j).wait_send()
        store_copy(0, j).wait()
        store_copy(1, j).wait()
        for s in range(SUBSTEPS):

            @pl.when(has_north)
            def _():
                halo_copy(s, 0, j).wait_send()

            @pl.when(has_south)
            def _():
                halo_copy(s, 1, j).wait_send()


def body(
    peers,
    analysis,
    copy_counts,
    spreading_coefficient,
    component_interaction,
    ocean_mask,
    measured_grid_location,
    measured_surface_reading,
    measured_inverse_variance,
):
    per_slot, comp, rows, lon = analysis.shape
    slots = copy_counts.shape[0]
    tiles = -(-lon // LANES)
    wide = tiles * LANES
    deep = -(-tiles * rows // LANES) * LANES
    rounds = radix_steps(peers)
    widest = max([size for _, size in rounds] + [1])
    f32 = jnp.float32
    vmem = pl.BlockSpec(memory_space=pltpu.VMEM)
    smem = pl.BlockSpec(memory_space=pltpu.SMEM)
    hbm = pl.BlockSpec(memory_space=pl.ANY)
    dma = pltpu.SemaphoreType.DMA
    obs = measured_grid_location.shape[0]
    fields, totals = pl.pallas_call(
        functools.partial(forecast_kernel, peers),
        out_shape=(
            jax.ShapeDtypeStruct((2, comp, rows, wide), f32),
            jax.ShapeDtypeStruct((2, 8, LANES), f32),
        ),
        in_specs=[smem, smem, hbm, vmem, vmem, vmem, vmem, vmem],
        out_specs=(hbm, vmem),
        scratch_shapes=[
            pltpu.VMEM((per_slot, comp, rows, lon), f32),
            pltpu.VMEM((comp, rows, lon), f32),
            pltpu.VMEM((comp, rows, lon), f32),
            pltpu.VMEM((3, 2, comp, wide), f32),
            pltpu.VMEM((SUBSTEPS, 2, comp, wide), f32),
            pltpu.VMEM((SUBSTEPS, comp, wide), f32),
            pltpu.VMEM((SUBSTEPS, comp, wide), f32),
            pltpu.VMEM((2, comp, rows, wide), f32),
            pltpu.VMEM((comp, rows, wide), f32),
            pltpu.VMEM((comp, rows, wide), f32),
            pltpu.VMEM((rows, wide), f32),
            pltpu.VMEM((rows, wide), f32),
            pltpu.VMEM((deep, LANES), f32),
            pltpu.VMEM((2, 8, LANES), f32),
            pltpu.VMEM((max(len(rounds), 1), widest, 2, 8, LANES), f32),
            dma((per_slot,)),
            dma((2,)),
            dma((2,)),
            dma((SUBSTEPS, 2, CHUNKS)),
            dma((SUBSTEPS, 2, CHUNKS)),
            dma((CHUNKS,)),
            dma((CHUNKS,)),
            dma((2, CHUNKS)),
            dma((2,)),
            dma((max(len(rounds), 1), widest)),
            dma((max(len(rounds), 1), widest)),
        ],
        compiler_params=pltpu.CompilerParams(
            collective_id=0, has_side_effects=True, vmem_limit_bytes=48 * 1024 * 1024
        ),
        cost_estimate=pl.CostEstimate(
            flops=2 * SUBSTEPS * comp * comp * rows * lon,
            bytes_accessed=6 * comp * rows * lon * 4,
            transcendentals=0,
        ),
    )(
        copy_counts,
        component_interaction,
        analysis,
        spreading_coefficient,
        ocean_mask,
        measured_grid_location.reshape(1, obs),
        measured_surface_reading.reshape(1, obs),
        measured_inverse_variance.reshape(1, obs),
    )
    bounds = jnp.cumsum(copy_counts)
    head = jnp.min(jnp.where(bounds > 0, bounds, slots))
    position = lax.axis_index("ens") * per_slot + jnp.arange(per_slot, dtype=jnp.int32)
    from_first = position < head
    predicted = jnp.where(
        from_first[:, None, None, None], fields[0, ..., :lon][None], fields[1, ..., :lon][None]
    )
    summed = jnp.where(from_first, totals[0, 0, 0], totals[1, 0, 0])
    return predicted, -0.5 * summed / (obs * peers)


def solution(mesh):
    in_specs = (
        P(("runs", "ens"), None, "space", None),
        P("runs"),
        P(("runs", "space"), None),
        P(),
        P(("runs", "space"), None),
        P(("runs", "space")),
        P(("runs", "space")),
        P(("runs", "space")),
    )
    out_specs = (P(("runs", "ens"), None, "space", None), P(("runs", "ens")))
    return jax.shard_map(
        functools.partial(body, mesh.shape["space"]),
        mesh=mesh,
        in_specs=in_specs,
        out_specs=out_specs,
        check_vma=False,
    )
```

time: 127 us -> 73.1 us (0.58)
  Pallas kernels: 0 us -> 60 us
  waiting for transfers between devices: 43 us -> 0 us
  blocking collectives: 19.6 us -> 0 us
  starting transfers between devices: 18.8 us -> 0 us
  between operations: 14.3 us -> 0.67 us
  local copies, waits for them, and re-layouts: 20.6 us -> 7.35 us
  matrix products: 8.65 us -> 0 us
  other arithmetic: 1.69 us -> 4.72 us
    pallas_call x0 -> x1, Pallas kernels: none -> 60 us  [body(): pl.pallas_call(functools.partial(forecast_kernel, peers), out_shape=(jax....]
    ppermute x6 -> x0, waiting for transfers between devices: 25.4 us -> none  [the longest x3 15.7 us: padded_2(): before = lax.ppermute(last, axis, up)]
    psum x1 -> x0, blocking collectives: 19.6 us -> none  [particle_likelihood(): summed = lax.psum(partial_value, 'space')]
    ppermute x6 -> x0, starting transfers between devices: 18.8 us -> none  [the longest x3 14.9 us: padded_2(): before = lax.ppermute(last, axis, up)]
    all_gather x1 -> x0, waiting for transfers between devices: 17 us -> none  [body(): everyone = lax.all_gather(analysis, 'ens', axis=0, tiled=True)]
    gather x2 -> x0, local copies, waits for them, and re-layouts: 8.96 us -> none  [the longest x1 6.22 us: particle_likelihood(): picked = jnp.take(surface, measured_grid_location, axis=1)]
    dot_general x3 -> x0, matrix products: 8.65 us -> none  [update(): jnp.einsum('ij,pjrc->pirc', component_interaction, centre, precision=lax....]
    another operation x1 -> x0, local copies, waits for them, and re-layouts: 7.68 us -> none  [particle_likelihood(): surface = fields[:, 0].reshape(per_slot, -1)]
  transfers between devices with their start and end apart: 7 -> 0, of which waited for: 7 -> 0; matrix products, arithmetic and copies ran while one was open for 2% -> 0% of each run, Pallas kernels for 0% -> 0%
where the time goes in v1:
time: 73.1 us; the launch traced here: 72.8 us
  Pallas kernels  60 us (82%)
  local copies, waits for them, and re-layouts  7.35 us (10%)
  other arithmetic  4.72 us (6%)
    pallas_call x1, Pallas kernels, body(): pl.pallas_call(functools.partial(forecast_kernel, peers), out_shape=(jax....  60 us
    unnamed x18, local copies, waits for them, and re-layouts  6.71 us
    div x1, other arithmetic, body(): return (predicted, -0.5 * summed / (obs * peers))  2.4 us

profile of v1, /device:TPU:0, one launch (start us, length us, event | category | flops | bytes accessed | tf_op | source)
XLA Modules:
  0.0 72.8 jit_solution(2609474859675666494)
XLA Ops:
  0.6 0.0 copy-start.8
  0.6 0.0 copy-start
  0.7 1.5 %copy-done = f32[2,8,8,3600]{3,2,1,0:T(8,128)S(1)} copy-done((f32[2,8,8,3600]{3,2,1,0:T(8,128)S(1)}, f32[2,8,8,3600]{3,2,1,0:T(8,128)}, u32[]{:S(2)}) %copy-start) | copy-done | bytes 1843224
  2.2 0.0 copy-start.1
  2.2 0.9 %copy-done.1 = f32[8,3600]{1,0:T(8,128)S(1)} copy-done((f32[8,3600]{1,0:T(8,128)S(1)}, f32[8,3600]{1,0:T(8,128)}, u32[]{:S(2)}) %copy-start.1) | copy-done | bytes 115224
  3.1 0.0 copy-start.2
  3.1 0.9 %copy-done.2 = s32[8,3600]{1,0:T(8,128)S(1)} copy-done((s32[8,3600]{1,0:T(8,128)S(1)}, s32[8,3600]{1,0:T(8,128)}, u32[]{:S(2)}) %copy-start.2) | copy-done | bytes 115224
  4.0 0.0 copy-start.3
  4.0 0.7 copy-done.3
  4.7 0.0 copy-start.4
  4.7 0.7 copy-done.4
  5.3 0.0 copy-start.5
  5.3 0.7 copy-done.5
  6.0 0.0 copy-start.6
  6.0 0.7 copy-done.6
  6.7 0.0 copy-start.7
  6.7 0.7 copy-done.7
  7.4 60.0 %shard_map.95 = (f32[2,8,8,3712]{3,2,1,0:T(8,128)S(1)}, f32[2,8,128]{2,1,0:T(8,128)S(1)}) custom-call(s32[4]{0:T(128)S(1)} %copy-done.7, f32[8,8]{1,0:T(8,128)S(1)} %copy-done.3, f32[2,8,8,3600]{3,2,1,0:T(8,128)S(1)} %copy-done, f32[8,3600]{1,0:T(8,128)S(1)} %copy-done.1, s32[8,3600]{1,0:T(8,128)S(1)} %copy-done.2, s32[1,512]{1,0:T(1,128)S(1)} %bitcast.12, ...), custom_call_target="tpu_custom_call" | custom-call | flops 11059200 | bytes 5529600 | tf_op jit(solution)/shard_map/pallas_call | solution.py:394
  67.4 0.5 fusion.1
  67.9 0.0 copy-done.8
  67.9 0.2 reduce-window.9
  68.1 0.7 fusion
  68.8 2.4 %select_multiply_fusion = (f32[2]{0:T(128)}, pred[2]{0:T(512)(128)(4,1)S(1)}) fusion(f32[]{:T(128)} %bitcast.8, f32[]{:T(128)} %bitcast.7, s32[]{:T(128)} %fusion, s32[]{:T(128)S(6)} %mul.4), kind=kLoop, calls=%fused_computation.5 | loop fusion | flops 8 | bytes 26 | tf_op jit(solution)/shard_map/div | solution.py:456
  71.2 0.1 slice_bitcast_fusion.1
  71.3 1.4 %broadcast_select_fusion = f32[2,8,8,3600]{3,2,1,0:T(8,128)} fusion(f32[8,8,3600]{2,1,0:T(8,128)S(1)} %get-tuple-element.9, f32[8,8,3600]{2,1,0:T(8,128)S(1)} %get-tuple-element.8, pred[2]{0:T(512)(128)(4,1)S(1)} %get-tuple-element.7), kind=kLoop, calls=%fused_computation | loop fusion | flops 460800 | bytes 3686402 | tf_op jit(solution)/shard_map/jit(_where)/select_n | solution.py:452
Async XLA Ops:
  0.6 67.3 %copy-start.8 = (s32[4]{0:T(128)S(1)}, s32[4]{0:T(128)}, u32[]{:S(2)}) copy-start(s32[4]{0:T(128)} %counts.1) | copy-start | bytes 52
  0.6 1.5 %copy-start = (f32[2,8,8,3600]{3,2,1,0:T(8,128)S(1)}, f32[2,8,8,3600]{3,2,1,0:T(8,128)}, u32[]{:S(2)}) copy-start(f32[2,8,8,3600]{3,2,1,0:T(8,128)} %analysis.1) | copy-start | bytes 5529604
  2.2 0.9 %copy-start.1 = (f32[8,3600]{1,0:T(8,128)S(1)}, f32[8,3600]{1,0:T(8,128)}, u32[]{:S(2)}) copy-start(f32[8,3600]{1,0:T(8,128)} %coef.1) | copy-start | bytes 345604
  3.1 0.9 %copy-start.2 = (s32[8,3600]{1,0:T(8,128)S(1)}, s32[8,3600]{1,0:T(8,128)}, u32[]{:S(2)}) copy-start(s32[8,3600]{1,0:T(8,128)} %mask.1) | copy-start | bytes 345604
  4.0 0.7 copy-start.3
  4.7 0.7 copy-start.4
  5.3 0.7 copy-start.5
  6.0 0.7 copy-start.6
  6.7 0.7 copy-start.7

commit v2 on v1

--- a/solution.py
+++ b/solution.py
@@ -10,6 +10,7 @@
 SUBSTEPS = 3
 CHUNKS = 4
 LANES = 128
+GROUP = 3
 MESH = pl.DeviceIdType.MESH
 
 
@@ -24,16 +25,23 @@
 
 def forecast_kernel(
     peers,
+    counts_hbm,
+    inter_hbm,
+    analysis,
+    coef_hbm,
+    mask_hbm,
+    loc_hbm,
+    reading_hbm,
+    inv_var_hbm,
+    out,
+    score,
     counts,
     inter,
-    analysis,
     coef,
     mask,
     loc,
     reading,
     inv_var,
-    out,
-    totals,
     raw,
     cand,
     taken,
@@ -56,18 +64,22 @@
     recv_sem,
     final_send,
     final_recv,
-    store_sem,
     pair_sem,
     sum_send,
     sum_recv,
 ):
     comp, rows, lon = analysis.shape[1:]
-    tiles = wet.shape[1] // LANES
+    wide = wet.shape[1]
+    width = GROUP * LANES
+    tiles = wide // LANES
+    groups = wide // width
     slots = counts.shape[0]
     per_slot = slots // 2
-    tail = lon - (tiles - 1) * LANES
-    half = (LANES - tail) // 2
-    bounds = [tiles * j // CHUNKS for j in range(CHUNKS + 1)]
+    full = lon // width
+    tail = lon - full * width
+    half = (wide - lon) // 2
+    rest = wide - lon - half
+    bounds = [groups * j // CHUNKS for j in range(CHUNKS + 1)]
     steps = radix_steps(peers)
 
     e = lax.axis_index("ens")
@@ -78,7 +90,21 @@
     loads = [
         pltpu.make_async_copy(analysis.at[p], raw.at[p], load_sem.at[p]) for p in range(per_slot)
     ]
-    for copy in loads:
+    small = [
+        pltpu.make_async_copy(src, dst, load_sem.at[per_slot + i])
+        for i, (src, dst) in enumerate(
+            (
+                (counts_hbm, counts),
+                (coef_hbm, coef),
+                (mask_hbm, mask),
+                (inter_hbm, inter),
+                (loc_hbm, loc),
+                (reading_hbm, reading),
+                (inv_var_hbm, inv_var),
+            )
+        )
+    ]
+    for copy in small[:3] + loads + small[3:]:
         copy.start()
 
     def digit_peers():
@@ -109,24 +135,26 @@
 
     def tail_of(load):
         return jnp.concatenate(
-            [load(lon - tail, lon), load(0, half), load(lon - (LANES - tail - half), lon)], axis=-1
+            [load(lon - tail, lon), load(0, half), load(lon - rest, lon)], axis=-1
         )
 
     def tile_loop(first, last, body):
         def step(k, carry):
-            body(k, pl.ds(pl.multiple_of(k * LANES, LANES), LANES))
+            body(k, pl.ds(pl.multiple_of(k * width, LANES), width))
             return carry
 
         lax.fori_loop(first, last, step, 0)
 
-    last = pl.ds((tiles - 1) * LANES, LANES)
+    last = pl.ds(full * width, width)
 
     def prepare(c, m, at):
         w = m.astype(jnp.float32)
         wet[:, at] = w
         wcoef[:, at] = w * c
 
-    tile_loop(0, tiles - 1, lambda k, at: prepare(coef[:, at], mask[:, at], at))
+    for copy in small[:3]:
+        copy.wait()
+    tile_loop(0, full, lambda k, at: prepare(coef[:, at], mask[:, at], at))
     prepare(
         tail_of(lambda a, b: coef[:, a:b]),
         tail_of(lambda a, b: mask[:, a:b].astype(jnp.float32)),
@@ -159,6 +187,8 @@
 
     for copy in loads:
         copy.wait()
+    for copy in small[3:]:
+        copy.wait()
 
     def pack_edges(p, slot):
         def put(load, at):
@@ -167,7 +197,7 @@
                 edges[slot, 0, c : c + 1, at] = v[0:1]
                 edges[slot, 1, c : c + 1, at] = v[rows - 1 : rows]
 
-        tile_loop(0, tiles - 1, lambda k, at: put(lambda c: raw[p, c, :, at], at))
+        tile_loop(0, full, lambda k, at: put(lambda c: raw[p, c, :, at], at))
         put(lambda c: tail_of(lambda a, b: raw[p, c, :, a:b]), last)
 
     pack_edges(their_row, 2)
@@ -188,7 +218,7 @@
     edge_copy.wait()
 
     def halo_copy(s, side, j):
-        at = pl.ds(bounds[j] * LANES, (bounds[j + 1] - bounds[j]) * LANES)
+        at = pl.ds(bounds[j] * width, (bounds[j + 1] - bounds[j]) * width)
         dst = south if side == 0 else north
         to = me - 1 if side == 0 else me + 1
         return pltpu.make_async_remote_copy(
@@ -224,17 +254,17 @@
         for c in range(comp):
             fields[0, c, :, at] = jnp.where(is_own, raw[own_row, c, :, at], taken[c, :, at])
 
-    tile_loop(0, tiles - 1, begin)
+    tile_loop(0, full, begin)
     for c in range(comp):
         fields[0, c, :, last] = tail_of(
             lambda a, b: jnp.where(is_own, raw[own_row, c, :, a:b], taken[c, :, a:b])
         )
 
-    lane = lax.broadcasted_iota(jnp.int32, (rows, LANES), 1)
-    row = lax.broadcasted_iota(jnp.int32, (rows, LANES), 0)
+    lane = lax.broadcasted_iota(jnp.int32, (rows, width), 1)
+    row = lax.broadcasted_iota(jnp.int32, (rows, width), 0)
 
     def final_copy(j):
-        at = pl.ds(bounds[j] * LANES, (bounds[j + 1] - bounds[j]) * LANES)
+        at = pl.ds(bounds[j] * width, (bounds[j + 1] - bounds[j]) * width)
         return pltpu.make_async_remote_copy(
             result.at[:, :, at],
             other.at[:, :, at],
@@ -244,13 +274,6 @@
             MESH,
         )
 
-    def store_copy(which, j):
-        at = pl.ds(bounds[j] * LANES, (bounds[j + 1] - bounds[j]) * LANES)
-        src, slot = (result, e) if which == 0 else (other, 1 - e)
-        return pltpu.make_async_copy(
-            src.at[:, :, at], out.at[slot, :, :, at], store_sem.at[which, j]
-        )
-
     for s in range(SUBSTEPS):
         src = fields.at[s % 2]
         dst = result if s == SUBSTEPS - 1 else fields.at[(s + 1) % 2]
@@ -265,21 +288,23 @@
                 halo_copy(s, 0, j).wait_recv()
 
             def advance(k, at):
-                before = pl.ds(pl.multiple_of(lax.rem(k + tiles - 1, tiles) * LANES, LANES), LANES)
-                after = pl.ds(pl.multiple_of(lax.rem(k + 1, tiles) * LANES, LANES), LANES)
+                before = pl.ds(pl.multiple_of(lax.rem(k * GROUP + tiles - 1, tiles) * LANES, LANES), LANES)
+                after = pl.ds(pl.multiple_of(lax.rem((k + 1) * GROUP, tiles) * LANES, LANES), LANES)
                 x = [src[c, :, at] for c in range(comp)]
                 w, wc = wet[:, at], wcoef[:, at]
                 for i in range(comp):
                     mixing = x[i]
                     for c in range(comp):
                         mixing = mixing + inter[i, c] * x[c]
+                    edge_l = pltpu.roll(src[i, :, before], 1, 1)
+                    edge_r = pltpu.roll(src[i, :, after], LANES - 1, 1)
                     left = jnp.where(
-                        lane == 0, pltpu.roll(src[i, :, before], 1, 1), pltpu.roll(x[i], 1, 1)
+                        lane == 0, jnp.concatenate([edge_l] * GROUP, 1), pltpu.roll(x[i], 1, 1)
                     )
                     right = jnp.where(
-                        lane == LANES - 1,
-                        pltpu.roll(src[i, :, after], LANES - 1, 1),
-                        pltpu.roll(x[i], LANES - 1, 1),
+                        lane == width - 1,
+                        jnp.concatenate([edge_r] * GROUP, 1),
+                        pltpu.roll(x[i], width - 1, 1),
                     )
                     up = jnp.where(row == 0, north[s, i : i + 1, at], pltpu.roll(x[i], 1, 0))
                     down = jnp.where(
@@ -291,14 +316,15 @@
                         send[s + 1, 0, i : i + 1, at] = v[0:1]
                         send[s + 1, 1, i : i + 1, at] = v[rows - 1 : rows]
                     elif i == 0:
-                        surface[pl.ds(pl.multiple_of(k * rows, rows), rows), :] = v
+                        for g in range(GROUP):
+                            to = pl.ds(pl.multiple_of((k * GROUP + g) * rows, rows), rows)
+                            surface[to, :] = v[:, g * LANES : (g + 1) * LANES]
 
             tile_loop(bounds[j], bounds[j + 1], advance)
             if s < SUBSTEPS - 1:
                 send_halo(s + 1, j)
             else:
                 final_copy(j).start()
-                store_copy(0, j).start()
 
     where = loc[...]
     band_row = sum((where >= lon * i).astype(jnp.int32) for i in range(1, rows))
@@ -347,15 +373,35 @@
         running = gather[r, 0]
         for q in range(1, size):
             running = running + gather[r, q]
-    totals[...] = running
+    dup = jnp.logical_or(
+        *(
+            jnp.logical_and(e == slot, copied)
+            for slot, copied in enumerate(
+                (
+                    sum((v <= 1).astype(jnp.int32) for v in sums) == first,
+                    sum((v <= slots - 2).astype(jnp.int32) for v in sums) == final,
+                )
+            )
+        )
+    )
+    scale = -0.5 / (obs * peers)
+    x, y = running[0, 0:1, 0:2], running[1, 0:1, 0:2]
+    own, far = jnp.where(e == 0, x, y), jnp.where(e == 0, y, x)
+    spot = lax.broadcasted_iota(jnp.int32, (1, 2), 1)
+    score[...] = scale * jnp.where(jnp.logical_or(spot == e, dup), own, far)
+
+    def choose(at, of):
+        for c in range(comp):
+            a, b = result[c, :, of], other[c, :, of]
+            out[e, c, :, at] = a
+            out[1 - e, c, :, at] = jnp.where(dup, a, b)
 
     for j in range(CHUNKS):
         final_copy(j).wait_recv()
-        store_copy(1, j).start()
+        tile_loop(bounds[j], min(bounds[j + 1], full), lambda k, at: choose(at, at))
+    choose(pl.ds(full * width, tail), pl.ds(full * width, tail))
     for j in range(CHUNKS):
         final_copy(j).wait_send()
-        store_copy(0, j).wait()
-        store_copy(1, j).wait()
         for s in range(SUBSTEPS):
 
             @pl.when(has_north)
@@ -380,26 +426,33 @@
 ):
     per_slot, comp, rows, lon = analysis.shape
     slots = copy_counts.shape[0]
-    tiles = -(-lon // LANES)
-    wide = tiles * LANES
+    width = GROUP * LANES
+    wide = -(-(lon + 2 * SUBSTEPS) // width) * width
+    tiles = wide // LANES
     deep = -(-tiles * rows // LANES) * LANES
     rounds = radix_steps(peers)
     widest = max([size for _, size in rounds] + [1])
     f32 = jnp.float32
     vmem = pl.BlockSpec(memory_space=pltpu.VMEM)
-    smem = pl.BlockSpec(memory_space=pltpu.SMEM)
-    hbm = pl.BlockSpec(memory_space=pl.ANY)
+    hbm = pl.BlockSpec(memory_space=pltpu.HBM)
     dma = pltpu.SemaphoreType.DMA
     obs = measured_grid_location.shape[0]
-    fields, totals = pl.pallas_call(
+    predicted, score = pl.pallas_call(
         functools.partial(forecast_kernel, peers),
         out_shape=(
-            jax.ShapeDtypeStruct((2, comp, rows, wide), f32),
-            jax.ShapeDtypeStruct((2, 8, LANES), f32),
+            jax.ShapeDtypeStruct(analysis.shape, f32),
+            jax.ShapeDtypeStruct((1, per_slot), f32),
         ),
-        in_specs=[smem, smem, hbm, vmem, vmem, vmem, vmem, vmem],
-        out_specs=(hbm, vmem),
+        in_specs=[hbm] * 8,
+        out_specs=(vmem, vmem),
         scratch_shapes=[
+            pltpu.SMEM(copy_counts.shape, jnp.int32),
+            pltpu.SMEM(component_interaction.shape, f32),
+            pltpu.VMEM((rows, lon), f32),
+            pltpu.VMEM((rows, lon), jnp.int32),
+            pltpu.VMEM((1, obs), jnp.int32),
+            pltpu.VMEM((1, obs), f32),
+            pltpu.VMEM((1, obs), f32),
             pltpu.VMEM((per_slot, comp, rows, lon), f32),
             pltpu.VMEM((comp, rows, lon), f32),
             pltpu.VMEM((comp, rows, lon), f32),
@@ -415,20 +468,19 @@
             pltpu.VMEM((deep, LANES), f32),
             pltpu.VMEM((2, 8, LANES), f32),
             pltpu.VMEM((max(len(rounds), 1), widest, 2, 8, LANES), f32),
-            dma((per_slot,)),
+            dma((per_slot + 7,)),
             dma((2,)),
             dma((2,)),
             dma((SUBSTEPS, 2, CHUNKS)),
             dma((SUBSTEPS, 2, CHUNKS)),
             dma((CHUNKS,)),
             dma((CHUNKS,)),
-            dma((2, CHUNKS)),
             dma((2,)),
             dma((max(len(rounds), 1), widest)),
             dma((max(len(rounds), 1), widest)),
         ],
         compiler_params=pltpu.CompilerParams(
-            collective_id=0, has_side_effects=True, vmem_limit_bytes=48 * 1024 * 1024
+            collective_id=0, has_side_effects=True, vmem_limit_bytes=64 * 1024 * 1024 - 65536
         ),
         cost_estimate=pl.CostEstimate(
             flops=2 * SUBSTEPS * comp * comp * rows * lon,
@@ -445,15 +497,7 @@
         measured_surface_reading.reshape(1, obs),
         measured_inverse_variance.reshape(1, obs),
     )
-    bounds = jnp.cumsum(copy_counts)
-    head = jnp.min(jnp.where(bounds > 0, bounds, slots))
-    position = lax.axis_index("ens") * per_slot + jnp.arange(per_slot, dtype=jnp.int32)
-    from_first = position < head
-    predicted = jnp.where(
-        from_first[:, None, None, None], fields[0, ..., :lon][None], fields[1, ..., :lon][None]
-    )
-    summed = jnp.where(from_first, totals[0, 0, 0], totals[1, 0, 0])
-    return predicted, -0.5 * summed / (obs * peers)
+    return predicted, score.reshape(per_slot)
 
 
 def solution(mesh):

time: 73.1 us -> 41 us (0.56)
  Pallas kernels: 60 us -> 36.8 us
  other arithmetic: 4.72 us -> 0 us
  local copies, waits for them, and re-layouts: 7.35 us -> 3.41 us
    pallas_call x1, Pallas kernels: 60 us -> 36.8 us  [body(): pl.pallas_call(functools.partial(forecast_kernel, peers), out_shape=(jax....]
    unnamed x18 -> x4, local copies, waits for them, and re-layouts: 6.71 us -> 3.41 us
    div x1 -> x0, other arithmetic: 2.4 us -> none  [body(): return (predicted, -0.5 * summed / (obs * peers))]
    select_n x1 -> x0, other arithmetic: 1.44 us -> none  [body(): jnp.where(from_first[:, None, None, None], fields[0, ..., :lon][None], fi...]
where the time goes in v2:
time: 41 us; the launch traced here: 40.8 us
  Pallas kernels  36.8 us (90%)
  local copies, waits for them, and re-layouts  3.41 us (8%)
  between operations  0.65 us (2%)
    pallas_call x1, Pallas kernels, body(): pl.pallas_call(functools.partial(forecast_kernel, peers), out_shape=(jax....  36.8 us
    unnamed x4, local copies, waits for them, and re-layouts  3.41 us

profile of v2, /device:TPU:0, one launch (start us, length us, event | category | flops | bytes accessed | tf_op | source)
XLA Modules:
  0.0 40.8 jit_solution(12471706896217829185)
XLA Ops:
  0.6 36.8 %shard_map.95 = (f32[2,8,8,3600]{3,2,1,0:T(8,128)}, f32[1,2]{1,0:T(1,128)}) custom-call(s32[4]{0:T(128)} %counts_hbm.1, f32[8,8]{1,0:T(8,128)} %inter_hbm.1, f32[2,8,8,3600]{3,2,1,0:T(8,128)} %analysis.1, f32[8,3600]{1,0:T(8,128)} %coef_hbm.1, s32[8,3600]{1,0:T(8,128)} %mask_hbm.1, s32[1,512]{1,0:T(1,128)} %bitcast.4, f32[1,512]{1,0:T(1,128)} %bitcast.5, ...), custom_call_target="tpu_custom_call" | custom-call | flops 11059200 | bytes 5529600 | tf_op jit(solution)/shard_map/pallas_call | solution.py:440
  37.4 0.0 copy-start
  37.4 2.9 %copy.12 = f32[2,8,8,3600]{3,2,1,0:T(8,128)} copy(f32[2,8,8,3600]{3,2,1,0:T(8,128)} %get-tuple-element.8) | data formatting | bytes 3686400
  40.3 0.0 copy-done
  40.3 0.5 %copy.13 = f32[2]{0:T(128)} copy(f32[2]{0:T(128)S(1)} %bitcast.7) | data formatting | bytes 16
Async XLA Ops:
  37.4 2.9 %copy-start = (f32[1,2]{1,0:T(1,128)S(1)}, f32[1,2]{1,0:T(1,128)}, u32[]{:S(2)}) copy-start(f32[1,2]{1,0:T(1,128)} %get-tuple-element.5) | copy-start | bytes 28

commit v3 on v2

--- a/solution.py
+++ b/solution.py
@@ -49,7 +49,9 @@
     send,
     north,
     south,
-    fields,
+    fields_a,
+    fields_b,
+    kmat,
     result,
     other,
     wet,
@@ -77,8 +79,9 @@
     per_slot = slots // 2
     full = lon // width
     tail = lon - full * width
-    half = (wide - lon) // 2
-    rest = wide - lon - half
+    ring = -(-(lon + 2 * SUBSTEPS) // LANES) * LANES
+    half = (ring - lon) // 2
+    rest = ring - lon - half
     bounds = [groups * j // CHUNKS for j in range(CHUNKS + 1)]
     steps = radix_steps(peers)
 
@@ -135,7 +138,7 @@
 
     def tail_of(load):
         return jnp.concatenate(
-            [load(lon - tail, lon), load(0, half), load(lon - rest, lon)], axis=-1
+            [load(lon - tail, lon), load(0, half), load(lon - rest, lon), load(0, wide - ring)][: 3 + (wide > ring)], axis=-1
         )
 
     def tile_loop(first, last, body):
@@ -161,6 +164,11 @@
         last,
     )
     surface[tiles * rows :, :] = jnp.zeros((surface.shape[0] - tiles * rows, LANES), jnp.float32)
+
+    if wide > ring:
+        for s in range(SUBSTEPS):
+            north[s, :, ring:] = jnp.zeros((comp, wide - ring), jnp.float32)
+            south[s, :, ring:] = jnp.zeros((comp, wide - ring), jnp.float32)
 
     @pl.when(jnp.logical_not(has_north))
     def _():
@@ -190,6 +198,20 @@
     for copy in small[3:]:
         copy.wait()
 
+    size = comp * rows
+    across = lax.broadcasted_iota(jnp.int32, (rows, size), 1)
+    down_row = lax.broadcasted_iota(jnp.int32, (rows, size), 0)
+    blocks = []
+    for i in range(comp):
+        block = jnp.zeros((rows, size), jnp.float32)
+        for c in range(comp):
+            block = jnp.where(across == c * rows + down_row, inter[i, c], block)
+        blocks.append(block)
+    coupling = jnp.concatenate(blocks, 0)
+    high = coupling.astype(jnp.bfloat16)
+    low = (coupling - high.astype(jnp.float32)).astype(jnp.bfloat16)
+    kmat[...] = jnp.concatenate([high, high, low], 1)
+
     def pack_edges(p, slot):
         def put(load, at):
             for c in range(comp):
@@ -218,7 +240,7 @@
     edge_copy.wait()
 
     def halo_copy(s, side, j):
-        at = pl.ds(bounds[j] * width, (bounds[j + 1] - bounds[j]) * width)
+        at = pl.ds(bounds[j] * width, min(bounds[j + 1] * width, ring) - bounds[j] * width)
         dst = south if side == 0 else north
         to = me - 1 if side == 0 else me + 1
         return pltpu.make_async_remote_copy(
@@ -252,11 +274,11 @@
 
     def begin(k, at):
         for c in range(comp):
-            fields[0, c, :, at] = jnp.where(is_own, raw[own_row, c, :, at], taken[c, :, at])
+            fields_a[c, :, at] = jnp.where(is_own, raw[own_row, c, :, at], taken[c, :, at])
 
     tile_loop(0, full, begin)
     for c in range(comp):
-        fields[0, c, :, last] = tail_of(
+        fields_a[c, :, last] = tail_of(
             lambda a, b: jnp.where(is_own, raw[own_row, c, :, a:b], taken[c, :, a:b])
         )
 
@@ -275,8 +297,8 @@
         )
 
     for s in range(SUBSTEPS):
-        src = fields.at[s % 2]
-        dst = result if s == SUBSTEPS - 1 else fields.at[(s + 1) % 2]
+        src = (fields_a, fields_b)[s % 2]
+        dst = result if s == SUBSTEPS - 1 else (fields_a, fields_b)[(s + 1) % 2]
         for j in range(CHUNKS):
 
             @pl.when(has_north)
@@ -288,14 +310,21 @@
                 halo_copy(s, 0, j).wait_recv()
 
             def advance(k, at):
-                before = pl.ds(pl.multiple_of(lax.rem(k * GROUP + tiles - 1, tiles) * LANES, LANES), LANES)
+                before = pl.ds(pl.multiple_of(lax.rem(k * GROUP + ring // LANES - 1, ring // LANES) * LANES, LANES), LANES)
                 after = pl.ds(pl.multiple_of(lax.rem((k + 1) * GROUP, tiles) * LANES, LANES), LANES)
                 x = [src[c, :, at] for c in range(comp)]
                 w, wc = wet[:, at], wcoef[:, at]
+                flat = jnp.concatenate(x, 0)
+                high = flat.astype(jnp.bfloat16)
+                low = (flat - high.astype(jnp.float32)).astype(jnp.bfloat16)
+                mixed = jnp.dot(
+                    kmat[...],
+                    jnp.concatenate([high, low, high], 0),
+                    preferred_element_type=jnp.float32,
+                )
+                done = []
                 for i in range(comp):
-                    mixing = x[i]
-                    for c in range(comp):
-                        mixing = mixing + inter[i, c] * x[c]
+                    mixing = x[i] + mixed[i * rows : (i + 1) * rows]
                     edge_l = pltpu.roll(src[i, :, before], 1, 1)
                     edge_r = pltpu.roll(src[i, :, after], LANES - 1, 1)
                     left = jnp.where(
@@ -310,7 +339,8 @@
                     down = jnp.where(
                         row == rows - 1, south[s, i : i + 1, at], pltpu.roll(x[i], rows - 1, 0)
                     )
-                    v = w * mixing + wc * ((up + down) + (left + right) - 4.0 * x[i])
+                    done.append(w * mixing + wc * ((up + down) + (left + right) - 4.0 * x[i]))
+                for i, v in enumerate(done):
                     dst[i, :, at] = v
                     if s < SUBSTEPS - 1:
                         send[s + 1, 0, i : i + 1, at] = v[0:1]
@@ -348,7 +378,30 @@
     pair_copy = pltpu.make_async_remote_copy(
         pair.at[e], pair.at[e], pair_sem.at[0], pair_sem.at[1], {"ens": 1 - e}, MESH
     )
+    dup = jnp.logical_or(
+        *(
+            jnp.logical_and(e == slot, copied)
+            for slot, copied in enumerate(
+                (
+                    sum((v <= 1).astype(jnp.int32) for v in sums) == first,
+                    sum((v <= slots - 2).astype(jnp.int32) for v in sums) == final,
+                )
+            )
+        )
+    )
+    def choose(at, of):
+        for c in range(comp):
+            a, b = result[c, :, of], other[c, :, of]
+            out[e, c, :, at] = a
+            out[1 - e, c, :, at] = jnp.where(dup, a, b)
+
+    def finish(chunks):
+        for j in chunks:
+            final_copy(j).wait_recv()
+            tile_loop(bounds[j], min(bounds[j + 1], full), lambda k, at: choose(at, at))
+
     pair_copy.start()
+    finish(range(CHUNKS - 1))
     pair_copy.wait()
     running = pair[...]
     for r, (stride, size) in enumerate(steps):
@@ -368,38 +421,20 @@
         ]
         for copy in copies:
             copy.start()
+        if r == 0:
+            finish([CHUNKS - 1])
+            choose(pl.ds(full * width, tail), pl.ds(full * width, tail))
         for copy in copies:
             copy.wait()
         running = gather[r, 0]
         for q in range(1, size):
             running = running + gather[r, q]
-    dup = jnp.logical_or(
-        *(
-            jnp.logical_and(e == slot, copied)
-            for slot, copied in enumerate(
-                (
-                    sum((v <= 1).astype(jnp.int32) for v in sums) == first,
-                    sum((v <= slots - 2).astype(jnp.int32) for v in sums) == final,
-                )
-            )
-        )
-    )
     scale = -0.5 / (obs * peers)
     x, y = running[0, 0:1, 0:2], running[1, 0:1, 0:2]
     own, far = jnp.where(e == 0, x, y), jnp.where(e == 0, y, x)
     spot = lax.broadcasted_iota(jnp.int32, (1, 2), 1)
     score[...] = scale * jnp.where(jnp.logical_or(spot == e, dup), own, far)
 
-    def choose(at, of):
-        for c in range(comp):
-            a, b = result[c, :, of], other[c, :, of]
-            out[e, c, :, at] = a
-            out[1 - e, c, :, at] = jnp.where(dup, a, b)
-
-    for j in range(CHUNKS):
-        final_copy(j).wait_recv()
-        tile_loop(bounds[j], min(bounds[j + 1], full), lambda k, at: choose(at, at))
-    choose(pl.ds(full * width, tail), pl.ds(full * width, tail))
     for j in range(CHUNKS):
         final_copy(j).wait_send()
         for s in range(SUBSTEPS):
@@ -460,7 +495,9 @@
             pltpu.VMEM((SUBSTEPS, 2, comp, wide), f32),
             pltpu.VMEM((SUBSTEPS, comp, wide), f32),
             pltpu.VMEM((SUBSTEPS, comp, wide), f32),
-            pltpu.VMEM((2, comp, rows, wide), f32),
+            pltpu.VMEM((comp, rows, wide), f32),
+            pltpu.VMEM((comp, rows, wide), f32),
+            pltpu.VMEM((comp * rows, 3 * comp * rows), jnp.bfloat16),
             pltpu.VMEM((comp, rows, wide), f32),
             pltpu.VMEM((comp, rows, wide), f32),
             pltpu.VMEM((rows, wide), f32),

time: 41 us -> 36.6 us (0.89)
  Pallas kernels: 36.8 us -> 32.4 us
    pallas_call x1, Pallas kernels: 36.8 us -> 32.4 us  [body(): pl.pallas_call(functools.partial(forecast_kernel, peers), out_shape=(jax....]
where the time goes in v3:
time: 36.6 us; the launch traced here: 36.5 us
  Pallas kernels  32.4 us (89%)
  local copies, waits for them, and re-layouts  3.41 us (9%)
  between operations  0.65 us (2%)
    pallas_call x1, Pallas kernels, body(): pl.pallas_call(functools.partial(forecast_kernel, peers), out_shape=(jax....  32.4 us
    unnamed x4, local copies, waits for them, and re-layouts  3.41 us

profile of v3, /device:TPU:0, one launch (start us, length us, event | category | flops | bytes accessed | tf_op | source)
XLA Modules:
  0.0 36.5 jit_solution(5110776221350050331)
XLA Ops:
  0.6 32.4 %shard_map.95 = (f32[2,8,8,3600]{3,2,1,0:T(8,128)}, f32[1,2]{1,0:T(1,128)}) custom-call(s32[4]{0:T(128)} %counts_hbm.1, f32[8,8]{1,0:T(8,128)} %inter_hbm.1, f32[2,8,8,3600]{3,2,1,0:T(8,128)} %analysis.1, f32[8,3600]{1,0:T(8,128)} %coef_hbm.1, s32[8,3600]{1,0:T(8,128)} %mask_hbm.1, s32[1,512]{1,0:T(1,128)} %bitcast.4, f32[1,512]{1,0:T(1,128)} %bitcast.5, ...), custom_call_target="tpu_custom_call" | custom-call | flops 11059200 | bytes 5529600 | tf_op jit(solution)/shard_map/pallas_call | solution.py:475
  33.0 0.0 copy-start
  33.1 2.9 %copy.12 = f32[2,8,8,3600]{3,2,1,0:T(8,128)} copy(f32[2,8,8,3600]{3,2,1,0:T(8,128)} %get-tuple-element.8) | data formatting | bytes 3686400
  35.9 0.0 copy-done
  36.0 0.5 %copy.13 = f32[2]{0:T(128)} copy(f32[2]{0:T(128)S(1)} %bitcast.7) | data formatting | bytes 16
Async XLA Ops:
  33.0 2.9 %copy-start = (f32[1,2]{1,0:T(1,128)S(1)}, f32[1,2]{1,0:T(1,128)}, u32[]{:S(2)}) copy-start(f32[1,2]{1,0:T(1,128)} %get-tuple-element.5) | copy-start | bytes 28
